TPU v7x, 128 devices: a whole 4x4x4 slice. The times are simulated.
128 devices in a mesh: wide: 8 (over y, core), narrow: 16 (over z, x).
Axes of the slice: x: 4, y: 4, z: 4, core: 2. Of those that a mesh axis runs over, the one named last changes fastest.
Arguments:
- positions: float32 [3, 1048576], P(None, ('wide', 'narrow')), may hold values from 0 to 1
- masses: float32 [1048576], P(('wide', 'narrow')), may hold values from 0.001 to 0.01
- node_mass: float32 [32768], P(('wide', 'narrow')), may hold values from 0.01 to 0.1
- node_centre: float32 [3, 32768], P(None, ('wide', 'narrow')), may hold values from 0 to 1
- node_quad: float32 [6, 32768], P(None, ('wide', 'narrow')), may hold values from -0.018 to 0.018
- local_leaves: int32 [8192, 8], P(('wide', 'narrow')), may hold values from 0 to 63
- node_lists: int32 [8192, 64], P(('wide', 'narrow')), may hold values from 0 to 32767
- export_block: int32 [16384], P(('wide', 'narrow')), may hold values from 0 to 63
- export_dest: int32 [16384, 1], P(('wide', 'narrow')), may hold values from 0 to 127; in each aligned block of 128 rows (0 to 127, 128 to 255, ...) at most 2 rows name the same one
- export_leaves: int32 [16384, 8], P(('wide', 'narrow')), may hold values from 0 to 63
Outputs:
- accel: float32 [3, 1048576], P(None, ('wide', 'narrow'))
Inputs may be any that keep to these rules, and one draw needn't show every extreme that they name: `export_dest`: in the exports of one device no destination appears more than 2 times, and some destination appears exactly 2 times.
All inputs are finite; a program needn't handle non-finite values.
Results may differ from a plain program's by a relative error of at most 0.00014.
Values sent between devices are 32-bit elements; how exact they have to be, the bound alone decides.
No kernel may reach another device: no remote copies, remote signals or barrier semaphores. Data moves between devices by JAX's collectives and lax.ppermute only.
A program may use at most 128 MiB of HBM per device.

v0:
```python
import functools

import jax
import jax.numpy as jnp
from jax import lax
from jax.experimental import pallas as pl
from jax.experimental.pallas import tpu as pltpu
from jax.sharding import PartitionSpec as P

ROWS = 128
LEAF_N = 8
LIST_N = 64
CAP = 2
BLK_DEV = 64
EXP_BLK = 128
AXES = ("wide", "narrow")
GROUP = 8
STEP = 16
TAIL = 8
NODE_FIELDS = 10
SOFTEN = 0.01

f32 = jnp.float32
bf16 = jnp.bfloat16
VMEM = pl.BlockSpec(memory_space=pltpu.VMEM)
SMEM = pl.BlockSpec(memory_space=pltpu.SMEM)
HBM = pl.BlockSpec(memory_space=pltpu.HBM)


def params(mib):
    return pltpu.CompilerParams(vmem_limit_bytes=mib * 2**20)


def split3(value):
    high = value.astype(bf16)
    rest = value - high.astype(f32)
    middle = rest.astype(bf16)
    low = (rest - middle.astype(f32)).astype(bf16)
    return high, middle, low


def dot(left, right):
    return jnp.dot(left, right, preferred_element_type=f32)


def fetch(sources, targets, sems):
    copies = [
        pltpu.make_async_copy(source, target, sems.at[number])
        for number, (source, target) in enumerate(zip(sources, targets))
    ]
    for copy in copies:
        copy.start()
    return copies


def node_rows(mass, centre, quad, nodes, devices):
    count = mass.shape[1]
    rows = count // 8
    fields = jnp.concatenate([mass, centre, quad, jnp.zeros((16 - NODE_FIELDS, count), f32)], axis=0)
    parts = [fields[:, part * rows : (part + 1) * rows] for part in range(8)]
    half = BLK_DEV // 2
    nodes = jnp.concatenate([nodes[0:half], nodes[half:]], axis=1)
    bits = rows.bit_length() - 1
    each = rows // GROUP
    share = (nodes & (rows - 1)) // each
    row = (share * devices + (nodes >> (bits + 3))) * each + (nodes & (each - 1))
    return jnp.concatenate(parts, axis=0).T, row, (nodes >> bits) & 7


def send_kernel(
    block_in, dest_in, leaf_in, pos_in, mass_in, node_mass_in, node_centre_in, node_quad_in, list_in,
    out_ref, slot_ref, pm_ref, row_ref, part_ref,
    block_ref, dest_ref, leaf_ref, pos_ref, mass_ref, node_mass_ref, node_centre_ref, node_quad_ref, list_ref,
    count_ref, ids_ref, sems,
):
    copies = fetch(
        (block_in, dest_in, leaf_in, pos_in, mass_in, node_mass_in, node_centre_in, node_quad_in, list_in),
        (
            block_ref, dest_ref, leaf_ref, pos_ref, mass_ref,
            node_mass_ref, node_centre_ref, node_quad_ref, list_ref,
        ),
        sems,
    )
    devices = out_ref.shape[0]
    shift = lax.axis_size("narrow").bit_length() - 1
    turn = lax.axis_index("narrow")
    out_ref[:, 0:CAP, 3:4, :] = jnp.full((devices, CAP, 1, ROWS), -1.0, f32)

    def clear(index, carry):
        for part in range(8):
            count_ref[index * 8 + part] = 0
        return carry

    lax.fori_loop(0, devices // 8, clear, 0)
    for copy in copies:
        copy.wait()
    table, row_ref[...], part_ref[...] = node_rows(
        node_mass_ref[...], node_centre_ref[...], node_quad_ref[...], list_ref[...], devices
    )
    each = table.shape[0] // GROUP
    for device in range(devices):
        member = (device & 1) + ((device >> 2) & 1) * 2 + ((device >> shift) & 1) * 4
        out_ref[device, CAP] = table[member * each : (member + 1) * each]
    size = pos_ref.shape[1]
    centre = jnp.sum(pos_ref[...], axis=1, keepdims=True) * (1.0 / size)
    moved = pos_ref[...] - centre
    square = jnp.sum(moved * moved, axis=0, keepdims=True)
    mass = mass_ref[...]
    pm_ref[:, 0:size] = jnp.concatenate([-2.0 * moved, square, mass * moved, mass], axis=0)
    pm_ref[:, size : size + ROWS] = jnp.broadcast_to(
        jnp.concatenate([centre, jnp.zeros((5, 1), f32)], axis=0), (8, ROWS)
    )
    ids_ref[...] = jnp.concatenate([leaf_ref[...].astype(f32)] * (ROWS // LEAF_N), axis=0).T

    def one(step, carry):
        for part in range(8):
            export = step * 8 + part
            dest = dest_ref[export]
            side, up, core = dest & 1, (dest >> 2) & 1, (dest >> shift) & 1
            base = dest - side - up * 4 - (core << shift)
            seen = count_ref[base]
            count_ref[base] = seen + 1
            member = (seen + turn) & (GROUP - 1)
            slot = seen >> 3
            target = base + (member & 1) + (member & 2) * 2 + ((member >> 2) << shift)
            distance = (side + up * 2 + core * 4) ^ member
            slot_ref[export] = target * CAP + slot
            slot_ref[EXP_BLK + export] = block_ref[export]
            start = pl.multiple_of(block_ref[export] * ROWS, ROWS)
            out_ref[target, slot, 0:3, :] = pos_ref[:, pl.ds(start, ROWS)]
            ids = ids_ref[pl.ds(export, 1), 0:LEAF_N]
            out_ref[target, slot, 3:4, 0:LEAF_N] = ids + (distance * BLK_DEV).astype(f32)
        return carry

    lax.fori_loop(0, EXP_BLK // 8, one, 0)


def send_blocks(devices, *arguments):
    lists = arguments[-1]
    half = (lists.shape[0] // 2, lists.shape[1] * 2)
    return pl.pallas_call(
        send_kernel,
        out_shape=(
            jax.ShapeDtypeStruct((devices, CAP + 1, 4, ROWS), f32),
            jax.ShapeDtypeStruct((2 * EXP_BLK,), jnp.int32),
            jax.ShapeDtypeStruct((8, BLK_DEV * ROWS + ROWS), f32),
            jax.ShapeDtypeStruct(half, jnp.int32),
            jax.ShapeDtypeStruct(half, jnp.int32),
        ),
        in_specs=[HBM] * len(arguments),
        out_specs=(VMEM, SMEM, VMEM, VMEM, VMEM),
        scratch_shapes=[
            pltpu.SMEM((EXP_BLK,), jnp.int32),
            pltpu.SMEM((EXP_BLK,), jnp.int32),
        ]
        + [pltpu.VMEM(value.shape, value.dtype) for value in arguments[2:]]
        + [
            pltpu.SMEM((devices,), jnp.int32),
            pltpu.VMEM((EXP_BLK, 128), f32),
            pltpu.SemaphoreType.DMA((len(arguments),)),
        ],
        compiler_params=params(56),
        name="send_blocks",
    )(*arguments)


def fill_tables(source_refs, table_ref, weight_ref):
    chunk = 32 if len(source_refs) == 1 else 8
    row = lax.broadcasted_iota(jnp.int32, (16, ROWS), 0)
    ones = jnp.where(row < 3, 1.0, 0.0).astype(bf16)

    def step(index, carry):
        start = pl.multiple_of(index * (chunk * ROWS), chunk * ROWS)
        for group, source_ref in enumerate(source_refs):
            rows = source_ref[:, pl.ds(start, chunk * ROWS)]
            for part in range(chunk):
                leaf = group * BLK_DEV + index * chunk + part
                high, middle, low = split3(rows[:, part * ROWS : (part + 1) * ROWS])
                half = [high, high, middle, middle, high, low, ones]
                table_ref[leaf] = jnp.concatenate(half + half, axis=0).T
                weight_ref[leaf] = jnp.concatenate([high, middle], axis=0)
        return carry

    lax.fori_loop(0, BLK_DEV // chunk, step, 0)


def pull_block(moved, leaves, table_ref, weight_ref, left):
    square = jnp.sum(moved * moved, axis=0, keepdims=True) + SOFTEN
    one = jnp.ones_like(square)
    none = jnp.zeros((4, ROWS), f32)
    high, middle, low = split3(jnp.concatenate([moved, one, none], axis=0))
    pieces = [piece.astype(f32) for piece in split3(square)]
    ends = jnp.concatenate(pieces + [none, none, none, one - one], axis=0).astype(bf16)
    half = jnp.concatenate([high, middle, high, middle, low, high, ends], axis=0)
    none = jnp.zeros_like(half)
    right = jnp.concatenate(
        [jnp.concatenate([half, none], axis=1), jnp.concatenate([none, half], axis=1)], axis=0
    )
    total = jnp.zeros((16, ROWS), f32)
    for pair in range(LEAF_N // 2):
        first, second = leaves[2 * pair], leaves[2 * pair + 1]
        spread = dot(jnp.where(left, table_ref[first], table_ref[second]), right)
        root = lax.rsqrt(spread)
        cubed = root * root * root
        high = cubed.astype(bf16)
        low = (cubed - high.astype(f32)).astype(bf16)
        for place, leaf in enumerate((first, second)):
            lanes = slice(place * ROWS, (place + 1) * ROWS)
            weight = weight_ref[leaf]
            total += dot(
                jnp.concatenate([weight, weight], axis=1),
                jnp.concatenate([high[:, lanes], low[:, lanes]], axis=0),
            )
    total = total[4:8] + total[12:16]
    return total[0:3] - moved * total[3:4]


def left_lanes():
    return lax.broadcasted_iota(jnp.int32, (ROWS, 128), 1) < 64


def remote_kernel(pos_ref, *refs):
    pm_refs = refs[:GROUP]
    out_ref, list_ref, leaf_ref, centre_ref, table_ref, weight_ref, sem = refs[GROUP:]
    devices = pos_ref.shape[0] // (CAP + 1)
    copy = pltpu.make_async_copy(pos_ref.at[:, 3], leaf_ref, sem)
    copy.start()
    size = BLK_DEV * ROWS
    for group, pm_ref in enumerate(pm_refs):
        centre_ref[group] = pm_ref[:, size : size + ROWS]
    fill_tables(pm_refs, table_ref, weight_ref)
    copy.wait()

    def note(index, found):
        for part in range(8):
            for slot in range(CAP):
                slot = (index * 8 + part) * (CAP + 1) + slot
                list_ref[found] = slot
                found = found + jnp.where(leaf_ref[slot, 0] >= 0.0, 1, 0)
        return found

    found = lax.fori_loop(0, devices // 8, note, 0)
    last = list_ref[jnp.maximum(found - 1, 0)]
    for place in range(TAIL):
        list_ref[found + place] = last
    left = left_lanes()

    def visits(start, count):
        results = []
        for place in range(count):
            slot = list_ref[start + place]
            leaves = [leaf_ref[slot, k].astype(jnp.int32) for k in range(LEAF_N)]
            moved = pos_ref[slot][0:3] - centre_ref[leaves[0] // BLK_DEV][0:3]
            results.append((slot, pull_block(moved, leaves, table_ref, weight_ref, left)))
        for slot, result in results:
            out_ref[slot // (CAP + 1), slot % (CAP + 1), 0:3] = result

    def step(index, carry):
        visits(index * STEP, STEP)
        return carry

    def tail(index, carry):
        visits(whole * STEP + index * TAIL, TAIL)
        return carry

    whole = found // STEP
    lax.fori_loop(0, whole, step, 0)
    lax.fori_loop(0, (found - whole * STEP + TAIL - 1) // TAIL, tail, 0)


def remote_pull(visitors, pms):
    devices = visitors.shape[0] // (CAP + 1)
    return pl.pallas_call(
        remote_kernel,
        out_shape=jax.ShapeDtypeStruct((devices, CAP, 4, ROWS), f32),
        in_specs=[VMEM] * (1 + GROUP),
        out_specs=VMEM,
        scratch_shapes=[
            pltpu.SMEM((devices * CAP + TAIL,), jnp.int32),
            pltpu.SMEM((visitors.shape[0], ROWS), f32),
            pltpu.VMEM((GROUP, 8, ROWS), f32),
            pltpu.VMEM((GROUP * BLK_DEV, ROWS, 128), bf16),
            pltpu.VMEM((GROUP * BLK_DEV, 16, ROWS), bf16),
            pltpu.SemaphoreType.DMA,
        ],
        compiler_params=params(28),
        cost_estimate=pl.CostEstimate(flops=32 * 10**9, bytes_accessed=10**7, transcendentals=16 * 10**6),
        name="remote_pull",
    )(visitors, *pms)


def node_sum(place, fields):
    mass, cx, cy, cz, qxx, qyy, qzz, qxy, qxz, qyz = fields
    x, y, z = place[0] - cx, place[1] - cy, place[2] - cz
    spread = x * x + y * y + (z * z + SOFTEN)
    quad_x = qxx * x + qxy * y + qxz * z
    quad_y = qxy * x + qyy * y + qyz * z
    quad_z = qxz * x + qyz * y + qzz * z
    root = lax.rsqrt(spread)
    inverse = root * root
    cubed = inverse * root
    fifth = cubed * inverse
    scalar = x * quad_x + y * quad_y + z * quad_z
    radial = mass * cubed + scalar * (fifth * (-2.5 * inverse))
    return radial * x + quad_x * fifth, radial * y + quad_y * fifth, radial * z + quad_z * fifth


NODE_PART = 16


def node_kernel(
    row_ref, part_ref, pm_ref, local_ref, *refs,
):
    half = BLK_DEV // 2
    share_refs, (out_ref, table_ref, weight_ref, spread_ref, gather_ref, nodes_ref) = refs[:GROUP], refs[GROUP : GROUP + 6]
    refs = refs[GROUP + 6 :]
    picked_refs, field_refs, place_refs, pull_refs = refs[0:2], refs[2:4], refs[4:6], refs[6:8]
    narrow = lax.axis_index("narrow")
    here = (narrow & 1) + ((narrow >> 2) & 1) * 2 + (lax.axis_index("wide") & 1) * 4
    devices, each = share_refs[0].shape[0], share_refs[0].shape[1]
    for distance, share_ref in enumerate(share_refs):
        first = pl.multiple_of((here ^ distance) * (devices * each), devices * each)
        for device in range(0, devices, 2):
            nodes_ref[pl.ds(first + device * each, 2 * each), :] = jnp.concatenate(
                [share_ref[device], share_ref[device + 1]], axis=0
            )
    fill_tables((pm_ref,), table_ref, weight_ref)
    left = left_lanes()

    row = lax.broadcasted_iota(jnp.int32, (ROWS, 128), 0)
    lane = lax.broadcasted_iota(jnp.int32, (ROWS, 128), 1)
    for along in range(3):
        inner = row & 63
        hit = (inner == along) | (inner == 16 + along) | (inner == 40 + along)
        hit = hit & ((row >> 6) == (lane >> 6))
        spread_ref[:, 128 * along : 128 * along + 128] = jnp.where(hit, -0.5, 0.0).astype(bf16)
        row16 = lax.broadcasted_iota(jnp.int32, (16, 256), 0)
        lane16 = lax.broadcasted_iota(jnp.int32, (16, 256), 1) & 127
        mine = row16 == along + 4 * (lane16 >> 6)
        gather_ref[along] = jnp.where(mine, 1.0, 0.0).astype(bf16)

    def pick(block, target, first, last):
        for node in range(first, last):
            target[pl.ds(node, 1), :] = nodes_ref[pl.ds(row_ref[block, node], 1), :]

    def lay_out(block, side):
        turned = picked_refs[side][...].T
        part = part_ref[pl.ds(block, 1), :]
        fields = turned[0:16]
        for number in range(1, 8):
            fields = jnp.where(part == number, turned[16 * number : 16 * number + 16], fields)
        centre = pm_ref[:, BLK_DEV * ROWS : BLK_DEV * ROWS + ROWS]
        rows = [-fields[0:1]] + [fields[k + 1 : k + 2] - centre[k : k + 1] for k in range(3)]
        rows += [fields[k : k + 1] for k in range(4, NODE_FIELDS)]
        for number, value in enumerate(rows):
            field_refs[side][number] = jnp.broadcast_to(value, (8, 128))
        both = jnp.where(left, table_ref[block], table_ref[block + half])
        place_refs[side][...] = dot(both, spread_ref[...])

    def compute(side, start):
        rows = [field_refs[side][number] for number in range(NODE_FIELDS)]
        halves = [
            node_sum([place_refs[side][at : at + 8, 128 * k : 128 * k + 128] for k in range(3)], rows)
            for at in range(start, start + NODE_PART, 8)
        ]
        for number in range(3):
            pull = jnp.concatenate([half_[number] for half_ in halves], axis=0)
            high = pull.astype(bf16)
            pull_refs[side][number, start : start + NODE_PART, 0:128] = high
            pull_refs[side][number, start : start + NODE_PART, 128:256] = (pull - high.astype(f32)).astype(bf16)

    def add_up(block, side):
        total = jnp.zeros((16, ROWS), f32)
        for number in range(3):
            total += lax.dot_general(
                gather_ref[number],
                pull_refs[side][number],
                (((1,), (1,)), ((), ())),
                preferred_element_type=f32,
            )
        out_ref[block, 0:3] = local_ref[block, 0:3] + total[0:3]
        out_ref[block + half, 0:3] = local_ref[block + half, 0:3] + total[4:7]

    pick(0, picked_refs[0], 0, 2 * LIST_N)
    pick(1, picked_refs[1], 0, 2 * LIST_N)
    lay_out(0, 0)

    def step(index, carry):
        for side in range(2):
            block = index * 2 + side
            other = 1 - side
            lay_out(jnp.minimum(block + 1, half - 1), other)
            add_up(jnp.maximum(block - 1, 0), other)
            ahead = jnp.minimum(block + 2, half - 1)
            for start in range(0, ROWS, NODE_PART):
                compute(side, start)
                pick(ahead, picked_refs[side], start, start + NODE_PART)
        return carry

    lax.fori_loop(0, half // 2, step, 0)
    add_up(half - 1, 1)


def node_pull(rows, parts, pm, local, shares):
    devices, each = shares[0].shape[0:2]
    return pl.pallas_call(
        node_kernel,
        out_shape=jax.ShapeDtypeStruct((BLK_DEV, 4, ROWS), f32),
        in_specs=[SMEM] + [VMEM] * (3 + GROUP),
        out_specs=VMEM,
        scratch_shapes=[
            pltpu.VMEM((BLK_DEV, ROWS, 128), bf16),
            pltpu.VMEM((BLK_DEV, 16, ROWS), bf16),
            pltpu.VMEM((ROWS, 3 * 128), bf16),
            pltpu.VMEM((3, 16, 256), bf16),
            pltpu.VMEM((GROUP * devices * each, 128), f32),
        ]
        + [pltpu.VMEM((2 * LIST_N, 128), f32)] * 2
        + [pltpu.VMEM((NODE_FIELDS, 8, 128), f32)] * 2
        + [pltpu.VMEM((ROWS, 3 * 128), f32)] * 2
        + [pltpu.VMEM((3, ROWS, 256), bf16)] * 2,
        compiler_params=params(14),
        cost_estimate=pl.CostEstimate(flops=12 * 10**9, bytes_accessed=4 * 10**6, transcendentals=10**6),
        name="node_pull",
    )(rows, parts, pm, local, *shares)


def local_kernel(leaf_ref, pm_ref, out_ref, table_ref, weight_ref):
    fill_tables((pm_ref,), table_ref, weight_ref)
    left = left_lanes()

    def step(index, carry):
        results = []
        for place in range(STEP):
            block = index * STEP + place
            start = pl.multiple_of(block * ROWS, ROWS)
            leaves = [leaf_ref[k, block] for k in range(LEAF_N)]
            moved = pm_ref[0:3, pl.ds(start, ROWS)] * -0.5
            results.append(pull_block(moved, leaves, table_ref, weight_ref, left))
        for place in range(STEP):
            out_ref[index * STEP + place, 0:3] = results[place]
        return carry

    lax.fori_loop(0, BLK_DEV // STEP, step, 0)


def local_pull(local_leaves, pm):
    return pl.pallas_call(
        local_kernel,
        out_shape=jax.ShapeDtypeStruct((BLK_DEV, 4, ROWS), f32),
        in_specs=[SMEM, VMEM],
        out_specs=VMEM,
        scratch_shapes=[
            pltpu.VMEM((BLK_DEV, ROWS, 128), bf16),
            pltpu.VMEM((BLK_DEV, 16, ROWS), bf16),
        ],
        compiler_params=params(10),
        cost_estimate=pl.CostEstimate(flops=16 * 10**9, bytes_accessed=10**6, transcendentals=8 * 10**6),
        name="local_pull",
    )(local_leaves, pm)


def add_kernel(slot_ref, own_ref, back_ref, out_ref, *sum_refs):
    parts = len(sum_refs)
    for part in range(1, parts):
        sum_refs[part][...] = jnp.zeros_like(sum_refs[part])
    sum_refs[0][...] = own_ref[...]

    def one(step, carry):
        for part in range(parts):
            export = step * parts + part
            block = slot_ref[EXP_BLK + export]
            sum_refs[part][block] += back_ref[slot_ref[export]]
        return carry

    lax.fori_loop(0, EXP_BLK // parts, one, 0)
    for block in range(BLK_DEV):
        total = sum_refs[0][block]
        for part in range(1, parts):
            total = total + sum_refs[part][block]
        out_ref[:, block * ROWS : (block + 1) * ROWS] = total[0:3]


def add_returned(slots, own, back):
    return pl.pallas_call(
        add_kernel,
        out_shape=jax.ShapeDtypeStruct((3, BLK_DEV * ROWS), f32),
        in_specs=[SMEM, VMEM, VMEM],
        out_specs=VMEM,
        scratch_shapes=[pltpu.VMEM((BLK_DEV, 4, ROWS), f32)] * 4,
        compiler_params=params(16),
        name="add_returned",
    )(slots, own, back)


def swap(values):
    return lax.all_to_all(values, AXES, split_axis=0, concat_axis=0, tiled=True)


def per_device(
    positions,
    masses,
    node_mass,
    node_centre,
    node_quad,
    local_leaves,
    node_lists,
    export_block,
    export_dest,
    export_leaves,
):
    groups = lax.axis_size("wide")
    members = lax.axis_size("narrow")
    devices = groups * members

    def same_core(value):
        flips = [[(i, i ^ flip) for i in range(members)] for flip in (1, 4, 5)]
        return [value] + [lax.ppermute(value, "narrow", flip) for flip in flips]

    def other_core(values):
        return values + [lax.ppermute(value, "wide", [(i, i ^ 1) for i in range(groups)]) for value in values]

    outgoing, slots, pm, rows, parts = send_blocks(
        devices,
        export_block,
        export_dest[:, 0],
        export_leaves.T,
        positions,
        masses[None],
        node_mass[None],
        node_centre,
        node_quad,
        node_lists,
    )
    arrived = swap(outgoing)
    pms = same_core(pm)
    local = local_pull(local_leaves.T, pm)
    arrived, local, pms = lax.optimization_barrier((arrived, local, pms))
    pms = other_core(pms)

    shares = same_core(arrived[:, CAP])
    visitors = arrived.reshape(devices * (CAP + 1), 4, ROWS)
    pulls = remote_pull(visitors, pms)
    pulls, local, shares = lax.optimization_barrier((pulls, local, shares))
    back = swap(pulls)
    shares = other_core(shares)
    own = node_pull(rows, parts, pm, local, shares)
    return add_returned(slots, own, back.reshape(devices * CAP, 4, ROWS))


def solution(mesh):
    both = P(AXES)
    lanes = P(None, AXES)
    rows = P(AXES, None)
    return jax.shard_map(
        per_device,
        mesh=mesh,
        in_specs=(lanes, both, both, lanes, lanes, rows, rows, both, rows, rows),
        out_specs=lanes,
        check_vma=False,
    )
```

profile of v0, /device:TPU:1, one launch (start us, length us, event | category | flops | bytes accessed | tf_op | source)
XLA Modules:
  0.0 92.3 jit_solution(1218678710638812468)
XLA Ops:
  0.0 4.4 %send_blocks.1 = (f32[128,3,4,128]{3,2,1,0:T(4,128)}, s32[256]{0:T(256)}, f32[8,8320]{1,0:T(8,128)}, s32[32,128]{1,0:T(8,128)}, s32[32,128]{1,0:T(8,128)}) custom-call(s32[128]{0:T(128)} %block_in.1, s32[128]{0:T(128)} %bitcast.15, s32[8,128]{1,0:T(8,128)} %bitcast.13, f32[3,8192]{1,0:T(4,128)} %pos_in.1, f32[1,8192]{1,0:T(1,128)} %bitcast.12, ...), custom_call_target="tpu_custom_call" | custom-call | tf_op jit(solution)/shard_map/send_blocks/pallas_call | solution.py:141
  4.5 2.1 %collective-permute-start = (f32[8,8320]{1,0:T(8,128)}, f32[8,8320]{1,0:T(8,128)S(1)}, u32[]{:S(2)}, u32[]{:S(2)}) collective-permute-start(f32[8,8320]{1,0:T(8,128)} %get-tuple-element.28.pm_ref.refs_0_), channel_id=1, source_target_pairs={{0,1},{1,0},{2,3},{3,2},{4,5},{5,4},{6,7},{7,6},{8,9},{9,8},{10,11... | collective-permute-start | bytes 798728 | tf_op jit(solution)/shard_map/ppermute | solution.py:518
  6.6 1.6 %collective-permute-start.1 = (f32[8,8320]{1,0:T(8,128)}, f32[8,8320]{1,0:T(8,128)S(1)}, u32[]{:S(2)}, u32[]{:S(2)}) collective-permute-start(f32[8,8320]{1,0:T(8,128)} %get-tuple-element.28.pm_ref.refs_0_), channel_id=1, source_target_pairs={{0,4},{1,5},{2,6},{3,7},{4,0},{5,1},{6,2},{7,3},{8,12},{9,13},{10,... | collective-permute-start | bytes 798728 | tf_op jit(solution)/shard_map/ppermute | solution.py:518
  8.2 0.0 collective-permute-start.2
  8.2 0.0 copy-start.1
  8.2 0.0 copy-start.4
  8.2 11.3 %all-to-all-start = ((f32[128,3,4,128]{3,2,1,0:T(4,128)}), f32[128,3,4,128]{3,2,1,0:T(4,128)S(1)}, u32[]{:S(2)}, u32[]{:S(2)}) async-start(f32[128,3,4,128]{3,2,1,0:T(4,128)} %get-tuple-element.26), calls=%async_computation | async-start | bytes 1572864 | tf_op jit(solution)/shard_map/all_to_all | solution.py:497
  19.5 0.0 copy-done.1
  19.5 0.0 copy-done.4
  19.6 11.2 %local_pull.1.local_ref = f32[64,4,128]{2,1,0:T(4,128)S(1)} custom-call(s32[8,64]{1,0:T(8,128)S(1)} %bitcast.11, f32[8,8320]{1,0:T(8,128)S(1)} %copy-done.1), custom_call_target="tpu_custom_call" | custom-call | flops 16000000000 | bytes 1000000 | tf_op jit(solution)/shard_map/local_pull/pallas_call | solution.py:448
  30.8 0.0 collective-permute-done.refs_1_
  30.8 0.0 collective-permute-done.1.refs_2_
  30.8 0.0 collective-permute-done.2.refs_3_
  30.8 5.5 %all-to-all-done = f32[128,3,4,128]{3,2,1,0:T(4,128)S(1)} async-done(((f32[128,3,4,128]{3,2,1,0:T(4,128)}), f32[128,3,4,128]{3,2,1,0:T(4,128)S(1)}, u32[]{:S(2)}, u32[]{:S(2)}) %all-to-all-start) | async-done | bytes 786464 | tf_op jit(solution)/shard_map/all_to_all | solution.py:497
  36.3 0.6 collective-permute-start.3
  37.0 0.0 collective-permute-start.4
  37.0 0.5 collective-permute-start.5
  37.5 0.0 collective-permute-start.6
  37.5 0.5 collective-permute-start.7
  38.0 0.1 collective-permute-done.3.refs_4_
  38.1 0.6 collective-permute-start.8
  38.7 0.0 collective-permute-done.4.refs_5_
  38.7 1.6 %collective-permute-start.9 = (f32[128,4,128]{2,1,0:T(4,128)S(1)}, f32[128,4,128]{2,1,0:T(4,128)S(1)}, u32[]{:S(2)}, u32[]{:S(2)}) collective-permute-start(f32[128,4,128]{2,1,0:T(4,128)S(1)} %slice_bitcast_fusion.refs_0_), channel_id=1, source_target_pairs={{0,5},{1,4},{2,7},{3,6},{4,1},{5,0},{6,3},{7,2},{8,13},{9,12},{10,... | collective-permute-start | bytes 786440 | tf_op jit(solution)/shard_map/ppermute | solution.py:518
  40.3 0.0 collective-permute-done.5.refs_6_
  40.3 0.0 collective-permute-done.6.refs_7_
  40.3 27.8 %remote_pull.1 = f32[128,2,4,128]{3,2,1,0:T(4,128)} custom-call(f32[384,4,128]{2,1,0:T(4,128)S(1)} %bitcast.10, f32[8,8320]{1,0:T(8,128)S(1)} %copy-done.1, f32[8,8320]{1,0:T(8,128)S(1)} %collective-permute-done.refs_1_, f32[8,8320]{1,0:T(8,128)S(1)} %collective-permute-done.1.refs_2_, f32[8,8320]{1,0:T(8,128)S(1)} %collective-permute-done.2.refs_3_, ...), custom_call_target="tpu_custom_call" | custom-call | flops 32000000000 | bytes 10000000 | tf_op jit(solution)/shard_map/remote_pull/pallas_call | solution.py:273
  68.1 0.0 copy-start.2
  68.1 0.0 copy-start.3
  68.1 0.0 collective-permute-done.7.refs_1_
  68.1 0.0 collective-permute-done.8.refs_2_
  68.2 0.0 collective-permute-done.9.refs_3_
  68.2 0.1 collective-permute-start.10
  68.3 0.5 collective-permute-start.11
  68.8 0.3 collective-permute-start.12
  69.0 0.2 collective-permute-start.13
  69.3 6.5 %all-to-all-start.1 = ((f32[128,2,4,128]{3,2,1,0:T(4,128)}), f32[128,2,4,128]{3,2,1,0:T(4,128)S(1)}, u32[]{:S(2)}, u32[]{:S(2)}) async-start(f32[128,2,4,128]{3,2,1,0:T(4,128)} %remote_pull.1), calls=%async_computation.1 | async-start | bytes 1048576 | tf_op jit(solution)/shard_map/all_to_all | solution.py:497
  75.8 0.0 collective-permute-done.10.refs_4_
  75.8 0.0 collective-permute-done.11.refs_5_
  75.8 0.0 collective-permute-done.12.refs_6_
  75.8 0.0 collective-permute-done.13.refs_7_
  75.8 0.0 copy-done.2
  75.8 0.0 copy-done.3
  75.8 8.9 %node_pull.1.own_ref = f32[64,4,128]{2,1,0:T(4,128)S(1)} custom-call(s32[32,128]{1,0:T(8,128)S(1)} %copy-done.2, s32[32,128]{1,0:T(8,128)S(1)} %copy-done.3, f32[8,8320]{1,0:T(8,128)S(1)} %copy-done.1, f32[64,4,128]{2,1,0:T(4,128)S(1)} %local_pull.1.local_ref, f32[128,4,128]{2,1,0:T(4,128)S(1)} %slice_bitcast_fusion.refs_0_, ...), custom_call_target="tpu_custom_call" | custom-call | flops 12000000000 | bytes 4000000 | tf_op jit(solution)/shard_map/node_pull/pallas_call | solution.py:406
  84.7 5.1 %all-to-all-done.1 = f32[128,2,4,128]{3,2,1,0:T(4,128)S(1)} async-done(((f32[128,2,4,128]{3,2,1,0:T(4,128)}), f32[128,2,4,128]{3,2,1,0:T(4,128)S(1)}, u32[]{:S(2)}, u32[]{:S(2)}) %all-to-all-start.1) | async-done | bytes 524320 | tf_op jit(solution)/shard_map/all_to_all | solution.py:497
  89.9 0.0 copy-start
  89.9 0.7 copy-done
  90.5 1.8 %add_returned.1 = f32[3,8192]{1,0:T(4,128)} custom-call(s32[256]{0:T(256)S(1)} %copy-done, f32[64,4,128]{2,1,0:T(4,128)S(1)} %node_pull.1.own_ref, f32[256,4,128]{2,1,0:T(4,128)S(1)} %bitcast.9), custom_call_target="tpu_custom_call" | custom-call | tf_op jit(solution)/shard_map/add_returned/pallas_call | solution.py:485
  (1 shorter events, 0.0 us)
Async XLA Ops:
  4.5 26.4 %collective-permute-start = (f32[8,8320]{1,0:T(8,128)}, f32[8,8320]{1,0:T(8,128)S(1)}, u32[]{:S(2)}, u32[]{:S(2)}) collective-permute-start(f32[8,8320]{1,0:T(8,128)} %get-tuple-element.28.pm_ref.refs_0_), channel_id=1, source_target_pairs={{0,1},{1,0},{2,3},{3,2},{4,5},{5,4},{6,7},{7,6},{8,9},{9,8},{10,11... | collective-permute-start | bytes 798728 | tf_op jit(solution)/shard_map/ppermute | solution.py:518
  6.6 24.2 %collective-permute-start.1 = (f32[8,8320]{1,0:T(8,128)}, f32[8,8320]{1,0:T(8,128)S(1)}, u32[]{:S(2)}, u32[]{:S(2)}) collective-permute-start(f32[8,8320]{1,0:T(8,128)} %get-tuple-element.28.pm_ref.refs_0_), channel_id=1, source_target_pairs={{0,4},{1,5},{2,6},{3,7},{4,0},{5,1},{6,2},{7,3},{8,12},{9,13},{10,... | collective-permute-start | bytes 798728 | tf_op jit(solution)/shard_map/ppermute | solution.py:518
  8.2 22.6 %collective-permute-start.2 = (f32[8,8320]{1,0:T(8,128)}, f32[8,8320]{1,0:T(8,128)S(1)}, u32[]{:S(2)}, u32[]{:S(2)}) collective-permute-start(f32[8,8320]{1,0:T(8,128)} %get-tuple-element.28.pm_ref.refs_0_), channel_id=1, source_target_pairs={{0,5},{1,4},{2,7},{3,6},{4,1},{5,0},{6,3},{7,2},{8,13},{9,12},{10,... | collective-permute-start | bytes 798728 | tf_op jit(solution)/shard_map/ppermute | solution.py:518
  8.2 11.3 %copy-start.1 = (f32[8,8320]{1,0:T(8,128)S(1)}, f32[8,8320]{1,0:T(8,128)}, u32[]{:S(2)}) copy-start(f32[8,8320]{1,0:T(8,128)} %get-tuple-element.28.pm_ref.refs_0_) | copy-start | bytes 798724
  8.2 11.3 %copy-start.4 = (s32[64,8]{0,1:T(8,128)S(1)}, s32[64,8]{0,1:T(8,128)}, u32[]{:S(2)}) copy-start(s32[64,8]{0,1:T(8,128)} %param.15) | copy-start | bytes 6148
  8.2 28.1 %all-to-all-start = ((f32[128,3,4,128]{3,2,1,0:T(4,128)}), f32[128,3,4,128]{3,2,1,0:T(4,128)S(1)}, u32[]{:S(2)}, u32[]{:S(2)}) async-start(f32[128,3,4,128]{3,2,1,0:T(4,128)} %get-tuple-element.26), calls=%async_computation | async-start | bytes 1572864 | tf_op jit(solution)/shard_map/all_to_all | solution.py:497
  36.3 1.8 %collective-permute-start.3 = (f32[8,8320]{1,0:T(8,128)S(1)}, f32[8,8320]{1,0:T(8,128)S(1)}, u32[]{:S(2)}, u32[]{:S(2)}) collective-permute-start(f32[8,8320]{1,0:T(8,128)S(1)} %copy-done.1), channel_id=1, source_target_pairs={{0,16},{16,0},{32,48},{48,32},{64,80},{80,64},{96,112},{112,96},{1... | collective-permute-start | bytes 798728 | tf_op jit(solution)/shard_map/ppermute | solution.py:521
  37.0 1.7 %collective-permute-start.4 = (f32[8,8320]{1,0:T(8,128)S(1)}, f32[8,8320]{1,0:T(8,128)S(1)}, u32[]{:S(2)}, u32[]{:S(2)}) collective-permute-start(f32[8,8320]{1,0:T(8,128)S(1)} %collective-permute-done.refs_1_), channel_id=1, source_target_pairs={{0,16},{16,0},{32,48},{48,32},{64,80},{80,64},{96,112},{112,96},{1... | collective-permute-start | bytes 798728 | tf_op jit(solution)/shard_map/ppermute | solution.py:521
  37.0 3.3 %collective-permute-start.5 = (f32[8,8320]{1,0:T(8,128)S(1)}, f32[8,8320]{1,0:T(8,128)S(1)}, u32[]{:S(2)}, u32[]{:S(2)}) collective-permute-start(f32[8,8320]{1,0:T(8,128)S(1)} %collective-permute-done.1.refs_2_), channel_id=1, source_target_pairs={{0,16},{16,0},{32,48},{48,32},{64,80},{80,64},{96,112},{112,96},{1... | collective-permute-start | bytes 798728 | tf_op jit(solution)/shard_map/ppermute | solution.py:521
  37.5 2.8 %collective-permute-start.6 = (f32[8,8320]{1,0:T(8,128)S(1)}, f32[8,8320]{1,0:T(8,128)S(1)}, u32[]{:S(2)}, u32[]{:S(2)}) collective-permute-start(f32[8,8320]{1,0:T(8,128)S(1)} %collective-permute-done.2.refs_3_), channel_id=1, source_target_pairs={{0,16},{16,0},{32,48},{48,32},{64,80},{80,64},{96,112},{112,96},{1... | collective-permute-start | bytes 798728 | tf_op jit(solution)/shard_map/ppermute | solution.py:521
  37.5 30.6 %collective-permute-start.7 = (f32[128,4,128]{2,1,0:T(4,128)S(1)}, f32[128,4,128]{2,1,0:T(4,128)S(1)}, u32[]{:S(2)}, u32[]{:S(2)}) collective-permute-start(f32[128,4,128]{2,1,0:T(4,128)S(1)} %slice_bitcast_fusion.refs_0_), channel_id=1, source_target_pairs={{0,1},{1,0},{2,3},{3,2},{4,5},{5,4},{6,7},{7,6},{8,9},{9,8},{10,11... | collective-permute-start | bytes 786440 | tf_op jit(solution)/shard_map/ppermute | solution.py:518
  38.1 30.0 %collective-permute-start.8 = (f32[128,4,128]{2,1,0:T(4,128)S(1)}, f32[128,4,128]{2,1,0:T(4,128)S(1)}, u32[]{:S(2)}, u32[]{:S(2)}) collective-permute-start(f32[128,4,128]{2,1,0:T(4,128)S(1)} %slice_bitcast_fusion.refs_0_), channel_id=1, source_target_pairs={{0,4},{1,5},{2,6},{3,7},{4,0},{5,1},{6,2},{7,3},{8,12},{9,13},{10,... | collective-permute-start | bytes 786440 | tf_op jit(solution)/shard_map/ppermute | solution.py:518
  38.7 29.5 %collective-permute-start.9 = (f32[128,4,128]{2,1,0:T(4,128)S(1)}, f32[128,4,128]{2,1,0:T(4,128)S(1)}, u32[]{:S(2)}, u32[]{:S(2)}) collective-permute-start(f32[128,4,128]{2,1,0:T(4,128)S(1)} %slice_bitcast_fusion.refs_0_), channel_id=1, source_target_pairs={{0,5},{1,4},{2,7},{3,6},{4,1},{5,0},{6,3},{7,2},{8,13},{9,12},{10,... | collective-permute-start | bytes 786440 | tf_op jit(solution)/shard_map/ppermute | solution.py:518
  68.1 7.7 %copy-start.2 = (s32[32,128]{1,0:T(8,128)S(1)}, s32[32,128]{1,0:T(8,128)}, u32[]{:S(2)}) copy-start(s32[32,128]{1,0:T(8,128)} %get-tuple-element.23.row_ref) | copy-start | bytes 49156
  68.1 7.7 %copy-start.3 = (s32[32,128]{1,0:T(8,128)S(1)}, s32[32,128]{1,0:T(8,128)}, u32[]{:S(2)}) copy-start(s32[32,128]{1,0:T(8,128)} %get-tuple-element.24.part_ref) | copy-start | bytes 49156
  68.2 7.6 %collective-permute-start.10 = (f32[128,4,128]{2,1,0:T(4,128)S(1)}, f32[128,4,128]{2,1,0:T(4,128)S(1)}, u32[]{:S(2)}, u32[]{:S(2)}) collective-permute-start(f32[128,4,128]{2,1,0:T(4,128)S(1)} %slice_bitcast_fusion.refs_0_), channel_id=1, source_target_pairs={{0,16},{16,0},{32,48},{48,32},{64,80},{80,64},{96,112},{112,96},{1... | collective-permute-start | bytes 786440 | tf_op jit(solution)/shard_map/ppermute | solution.py:521
  68.3 7.5 %collective-permute-start.11 = (f32[128,4,128]{2,1,0:T(4,128)S(1)}, f32[128,4,128]{2,1,0:T(4,128)S(1)}, u32[]{:S(2)}, u32[]{:S(2)}) collective-permute-start(f32[128,4,128]{2,1,0:T(4,128)S(1)} %collective-permute-done.7.refs_1_), channel_id=1, source_target_pairs={{0,16},{16,0},{32,48},{48,32},{64,80},{80,64},{96,112},{112,96},{1... | collective-permute-start | bytes 786440 | tf_op jit(solution)/shard_map/ppermute | solution.py:521
  68.8 7.0 %collective-permute-start.12 = (f32[128,4,128]{2,1,0:T(4,128)S(1)}, f32[128,4,128]{2,1,0:T(4,128)S(1)}, u32[]{:S(2)}, u32[]{:S(2)}) collective-permute-start(f32[128,4,128]{2,1,0:T(4,128)S(1)} %collective-permute-done.8.refs_2_), channel_id=1, source_target_pairs={{0,16},{16,0},{32,48},{48,32},{64,80},{80,64},{96,112},{112,96},{1... | collective-permute-start | bytes 786440 | tf_op jit(solution)/shard_map/ppermute | solution.py:521
  69.0 6.8 %collective-permute-start.13 = (f32[128,4,128]{2,1,0:T(4,128)S(1)}, f32[128,4,128]{2,1,0:T(4,128)S(1)}, u32[]{:S(2)}, u32[]{:S(2)}) collective-permute-start(f32[128,4,128]{2,1,0:T(4,128)S(1)} %collective-permute-done.9.refs_3_), channel_id=1, source_target_pairs={{0,16},{16,0},{32,48},{48,32},{64,80},{80,64},{96,112},{112,96},{1... | collective-permute-start | bytes 786440 | tf_op jit(solution)/shard_map/ppermute | solution.py:521
  69.3 20.6 %all-to-all-start.1 = ((f32[128,2,4,128]{3,2,1,0:T(4,128)}), f32[128,2,4,128]{3,2,1,0:T(4,128)S(1)}, u32[]{:S(2)}, u32[]{:S(2)}) async-start(f32[128,2,4,128]{3,2,1,0:T(4,128)} %remote_pull.1), calls=%async_computation.1 | async-start | bytes 1048576 | tf_op jit(solution)/shard_map/all_to_all | solution.py:497
  89.9 0.7 copy-start
where the time goes:
time: 93.7 us; the launch traced here: 92.3 us
  Pallas kernels  54.2 us (58%)
  starting transfers between devices  26.4 us (28%)
  waiting for transfers between devices  10.8 us (12%)
    pallas_call x1, Pallas kernels, remote_pull(): pl.pallas_call(remote_kernel, out_shape=jax.ShapeDtypeStruct((devices, CA...  27.8 us
    all_to_all x2, starting transfers between devices, swap(): return lax.all_to_all(values, AXES, split_axis=0, concat_axis=0, tiled=True)  17.8 us
    pallas_call x1, Pallas kernels, local_pull(): pl.pallas_call(local_kernel, out_shape=jax.ShapeDtypeStruct((BLK_DEV, 4,...  11.2 us
    all_to_all x2, waiting for transfers between devices, swap(): return lax.all_to_all(values, AXES, split_axis=0, concat_axis=0, tiled=True)  10.6 us
    pallas_call x1, Pallas kernels, node_pull(): pl.pallas_call(node_kernel, out_shape=jax.ShapeDtypeStruct((BLK_DEV, 4, R...  8.93 us
    ppermute x6, starting transfers between devices, same_core(): return [value] + [lax.ppermute(value, 'narrow', flip) for flip in flips]  6.34 us
    pallas_call x1, Pallas kernels, send_blocks(): pl.pallas_call(send_kernel, out_shape=(jax.ShapeDtypeStruct((devices, CAP...  4.45 us
    ppermute x8, starting transfers between devices, other_core(): lax.ppermute(value, 'wide', [(i, i ^ 1) for i in range(groups)])  2.25 us
  transfers between devices with their start and end apart: 16, of which 3 were waited for; matrix products, arithmetic and copies ran while one was open for 0% of the time, Pallas kernels for 52%

commit v1 on v0

--- a/solution.py
+++ b/solution.py
@@ -17,6 +17,7 @@
 GROUP = 8
 STEP = 16
 TAIL = 8
+REMOTE_STEPS = (32, 16, 8)
 NODE_FIELDS = 10
 SOFTEN = 0.01
 
@@ -255,17 +256,17 @@
         for slot, result in results:
             out_ref[slot // (CAP + 1), slot % (CAP + 1), 0:3] = result
 
-    def step(index, carry):
-        visits(index * STEP, STEP)
-        return carry
-
-    def tail(index, carry):
-        visits(whole * STEP + index * TAIL, TAIL)
-        return carry
-
-    whole = found // STEP
-    lax.fori_loop(0, whole, step, 0)
-    lax.fori_loop(0, (found - whole * STEP + TAIL - 1) // TAIL, tail, 0)
+    done = 0
+    for count in REMOTE_STEPS:
+        left_over = found - done
+        steps = left_over // count if count > TAIL else (left_over + count - 1) // count
+
+        def step(index, carry, start=done, count=count):
+            visits(start + index * count, count)
+            return carry
+
+        lax.fori_loop(0, steps, step, 0)
+        done = done + steps * count
 
 
 def remote_pull(visitors, pms):

time: 93.7 us -> 93.8 us (level)
  Pallas kernels: 54.2 us -> 49.9 us
  starting transfers between devices: 26.4 us -> 30.6 us
    pallas_call x1, Pallas kernels: 27.8 us -> 23.5 us  [remote_pull(): pl.pallas_call(remote_kernel, out_shape=jax.ShapeDtypeStruct((devices, CA...]
    all_to_all x2, starting transfers between devices: 17.8 us -> 21.3 us  [swap(): return lax.all_to_all(values, AXES, split_axis=0, concat_axis=0, tiled=True)]
  transfers between devices with their start and end apart: 16 -> 16, of which waited for: 3 -> 3; matrix products, arithmetic and copies ran while one was open for 0% -> 0% of each run, Pallas kernels for 52% -> 47%
where the time goes in v1:
time: 93.8 us; the launch traced here: 92.2 us
  Pallas kernels  49.9 us (53%)
  starting transfers between devices  30.6 us (33%)
  waiting for transfers between devices  10.8 us (12%)
    pallas_call x1, Pallas kernels, remote_pull(): pl.pallas_call(remote_kernel, out_shape=jax.ShapeDtypeStruct((devices, CA...  23.5 us
    all_to_all x2, starting transfers between devices, swap(): return lax.all_to_all(values, AXES, split_axis=0, concat_axis=0, tiled=True)  21.3 us
    pallas_call x1, Pallas kernels, local_pull(): pl.pallas_call(local_kernel, out_shape=jax.ShapeDtypeStruct((BLK_DEV, 4,...  11.2 us
    all_to_all x2, waiting for transfers between devices, swap(): return lax.all_to_all(values, AXES, split_axis=0, concat_axis=0, tiled=True)  10.6 us
    pallas_call x1, Pallas kernels, node_pull(): pl.pallas_call(node_kernel, out_shape=jax.ShapeDtypeStruct((BLK_DEV, 4, R...  8.92 us
    ppermute x6, starting transfers between devices, same_core(): return [value] + [lax.ppermute(value, 'narrow', flip) for flip in flips]  6.34 us
    pallas_call x1, Pallas kernels, send_blocks(): pl.pallas_call(send_kernel, out_shape=(jax.ShapeDtypeStruct((devices, CAP...  4.45 us
    ppermute x8, starting transfers between devices, other_core(): lax.ppermute(value, 'wide', [(i, i ^ 1) for i in range(groups)])  2.88 us
  transfers between devices with their start and end apart: 16, of which 3 were waited for; matrix products, arithmetic and copies ran while one was open for 0% of the time, Pallas kernels for 47%

profile of v1, /device:TPU:1, one launch (start us, length us, event | category | flops | bytes accessed | tf_op | source)
XLA Modules:
  0.0 92.2 jit_solution(14673210492239084872)
XLA Ops:
  0.0 4.4 %send_blocks.1 = (f32[128,3,4,128]{3,2,1,0:T(4,128)}, s32[256]{0:T(256)}, f32[8,8320]{1,0:T(8,128)}, s32[32,128]{1,0:T(8,128)}, s32[32,128]{1,0:T(8,128)}) custom-call(s32[128]{0:T(128)} %block_in.1, s32[128]{0:T(128)} %bitcast.15, s32[8,128]{1,0:T(8,128)} %bitcast.13, f32[3,8192]{1,0:T(4,128)} %pos_in.1, f32[1,8192]{1,0:T(1,128)} %bitcast.12, ...), custom_call_target="tpu_custom_call" | custom-call | tf_op jit(solution)/shard_map/send_blocks/pallas_call | solution.py:142
  4.5 2.1 %collective-permute-start = (f32[8,8320]{1,0:T(8,128)}, f32[8,8320]{1,0:T(8,128)S(1)}, u32[]{:S(2)}, u32[]{:S(2)}) collective-permute-start(f32[8,8320]{1,0:T(8,128)} %get-tuple-element.28.pm_ref.refs_0_), channel_id=1, source_target_pairs={{0,1},{1,0},{2,3},{3,2},{4,5},{5,4},{6,7},{7,6},{8,9},{9,8},{10,11... | collective-permute-start | bytes 798728 | tf_op jit(solution)/shard_map/ppermute | solution.py:519
  6.6 1.6 %collective-permute-start.1 = (f32[8,8320]{1,0:T(8,128)}, f32[8,8320]{1,0:T(8,128)S(1)}, u32[]{:S(2)}, u32[]{:S(2)}) collective-permute-start(f32[8,8320]{1,0:T(8,128)} %get-tuple-element.28.pm_ref.refs_0_), channel_id=1, source_target_pairs={{0,4},{1,5},{2,6},{3,7},{4,0},{5,1},{6,2},{7,3},{8,12},{9,13},{10,... | collective-permute-start | bytes 798728 | tf_op jit(solution)/shard_map/ppermute | solution.py:519
  8.2 0.0 collective-permute-start.2
  8.2 0.0 copy-start.1
  8.2 0.0 copy-start.4
  8.2 11.3 %all-to-all-start = ((f32[128,3,4,128]{3,2,1,0:T(4,128)}), f32[128,3,4,128]{3,2,1,0:T(4,128)S(1)}, u32[]{:S(2)}, u32[]{:S(2)}) async-start(f32[128,3,4,128]{3,2,1,0:T(4,128)} %get-tuple-element.26), calls=%async_computation | async-start | bytes 1572864 | tf_op jit(solution)/shard_map/all_to_all | solution.py:498
  19.5 0.0 copy-done.1
  19.5 0.0 copy-done.4
  19.6 11.2 %local_pull.1.local_ref = f32[64,4,128]{2,1,0:T(4,128)S(1)} custom-call(s32[8,64]{1,0:T(8,128)S(1)} %bitcast.11, f32[8,8320]{1,0:T(8,128)S(1)} %copy-done.1), custom_call_target="tpu_custom_call" | custom-call | flops 16000000000 | bytes 1000000 | tf_op jit(solution)/shard_map/local_pull/pallas_call | solution.py:449
  30.8 0.0 collective-permute-done.refs_1_
  30.8 0.0 collective-permute-done.1.refs_2_
  30.8 0.0 collective-permute-done.2.refs_3_
  30.8 5.5 %all-to-all-done = f32[128,3,4,128]{3,2,1,0:T(4,128)S(1)} async-done(((f32[128,3,4,128]{3,2,1,0:T(4,128)}), f32[128,3,4,128]{3,2,1,0:T(4,128)S(1)}, u32[]{:S(2)}, u32[]{:S(2)}) %all-to-all-start) | async-done | bytes 786464 | tf_op jit(solution)/shard_map/all_to_all | solution.py:498
  36.3 0.6 collective-permute-start.3
  37.0 0.0 collective-permute-start.4
  37.0 0.5 collective-permute-start.5
  37.5 0.0 collective-permute-start.6
  37.5 0.5 collective-permute-start.7
  38.0 0.1 collective-permute-done.3.refs_4_
  38.1 0.6 collective-permute-start.8
  38.7 0.0 collective-permute-done.4.refs_5_
  38.7 1.6 %collective-permute-start.9 = (f32[128,4,128]{2,1,0:T(4,128)S(1)}, f32[128,4,128]{2,1,0:T(4,128)S(1)}, u32[]{:S(2)}, u32[]{:S(2)}) collective-permute-start(f32[128,4,128]{2,1,0:T(4,128)S(1)} %slice_bitcast_fusion.refs_0_), channel_id=1, source_target_pairs={{0,5},{1,4},{2,7},{3,6},{4,1},{5,0},{6,3},{7,2},{8,13},{9,12},{10,... | collective-permute-start | bytes 786440 | tf_op jit(solution)/shard_map/ppermute | solution.py:519
  40.3 0.0 collective-permute-done.5.refs_6_
  40.3 0.0 collective-permute-done.6.refs_7_
  40.3 23.5 %remote_pull.1 = f32[128,2,4,128]{3,2,1,0:T(4,128)} custom-call(f32[384,4,128]{2,1,0:T(4,128)S(1)} %bitcast.10, f32[8,8320]{1,0:T(8,128)S(1)} %copy-done.1, f32[8,8320]{1,0:T(8,128)S(1)} %collective-permute-done.refs_1_, f32[8,8320]{1,0:T(8,128)S(1)} %collective-permute-done.1.refs_2_, f32[8,8320]{1,0:T(8,128)S(1)} %collective-permute-done.2.refs_3_, ...), custom_call_target="tpu_custom_call" | custom-call | flops 32000000000 | bytes 10000000 | tf_op jit(solution)/shard_map/remote_pull/pallas_call | solution.py:274
  63.8 0.0 copy-start.2
  63.8 0.0 copy-start.3
  63.8 0.0 collective-permute-done.7.refs_1_
  63.8 0.0 collective-permute-done.8.refs_2_
  63.8 0.0 collective-permute-done.9.refs_3_
  63.8 1.1 %collective-permute-start.10 = (f32[128,4,128]{2,1,0:T(4,128)S(1)}, f32[128,4,128]{2,1,0:T(4,128)S(1)}, u32[]{:S(2)}, u32[]{:S(2)}) collective-permute-start(f32[128,4,128]{2,1,0:T(4,128)S(1)} %slice_bitcast_fusion.refs_0_), channel_id=1, source_target_pairs={{0,16},{16,0},{32,48},{48,32},{64,80},{80,64},{96,112},{112,96},{1... | collective-permute-start | bytes 786440 | tf_op jit(solution)/shard_map/ppermute | solution.py:522
  65.0 0.1 collective-permute-start.11
  65.0 0.4 collective-permute-start.12
  65.5 0.1 collective-permute-start.13
  65.6 10.0 %all-to-all-start.1 = ((f32[128,2,4,128]{3,2,1,0:T(4,128)}), f32[128,2,4,128]{3,2,1,0:T(4,128)S(1)}, u32[]{:S(2)}, u32[]{:S(2)}) async-start(f32[128,2,4,128]{3,2,1,0:T(4,128)} %remote_pull.1), calls=%async_computation.1 | async-start | bytes 1048576 | tf_op jit(solution)/shard_map/all_to_all | solution.py:498
  75.6 0.0 collective-permute-done.10.refs_4_
  75.6 0.0 collective-permute-done.11.refs_5_
  75.6 0.0 collective-permute-done.12.refs_6_
  75.6 0.0 collective-permute-done.13.refs_7_
  75.7 0.0 copy-done.2
  75.7 0.0 copy-done.3
  75.7 8.9 %node_pull.1.own_ref = f32[64,4,128]{2,1,0:T(4,128)S(1)} custom-call(s32[32,128]{1,0:T(8,128)S(1)} %copy-done.2, s32[32,128]{1,0:T(8,128)S(1)} %copy-done.3, f32[8,8320]{1,0:T(8,128)S(1)} %copy-done.1, f32[64,4,128]{2,1,0:T(4,128)S(1)} %local_pull.1.local_ref, f32[128,4,128]{2,1,0:T(4,128)S(1)} %slice_bitcast_fusion.refs_0_, ...), custom_call_target="tpu_custom_call" | custom-call | flops 12000000000 | bytes 4000000 | tf_op jit(solution)/shard_map/node_pull/pallas_call | solution.py:407
  84.6 5.1 %all-to-all-done.1 = f32[128,2,4,128]{3,2,1,0:T(4,128)S(1)} async-done(((f32[128,2,4,128]{3,2,1,0:T(4,128)}), f32[128,2,4,128]{3,2,1,0:T(4,128)S(1)}, u32[]{:S(2)}, u32[]{:S(2)}) %all-to-all-start.1) | async-done | bytes 524320 | tf_op jit(solution)/shard_map/all_to_all | solution.py:498
  89.7 0.0 copy-start
  89.7 0.7 copy-done
  90.4 1.8 %add_returned.1 = f32[3,8192]{1,0:T(4,128)} custom-call(s32[256]{0:T(256)S(1)} %copy-done, f32[64,4,128]{2,1,0:T(4,128)S(1)} %node_pull.1.own_ref, f32[256,4,128]{2,1,0:T(4,128)S(1)} %bitcast.9), custom_call_target="tpu_custom_call" | custom-call | tf_op jit(solution)/shard_map/add_returned/pallas_call | solution.py:486
  (1 shorter events, 0.0 us)
Async XLA Ops:
  4.5 26.4 %collective-permute-start = (f32[8,8320]{1,0:T(8,128)}, f32[8,8320]{1,0:T(8,128)S(1)}, u32[]{:S(2)}, u32[]{:S(2)}) collective-permute-start(f32[8,8320]{1,0:T(8,128)} %get-tuple-element.28.pm_ref.refs_0_), channel_id=1, source_target_pairs={{0,1},{1,0},{2,3},{3,2},{4,5},{5,4},{6,7},{7,6},{8,9},{9,8},{10,11... | collective-permute-start | bytes 798728 | tf_op jit(solution)/shard_map/ppermute | solution.py:519
  6.6 24.2 %collective-permute-start.1 = (f32[8,8320]{1,0:T(8,128)}, f32[8,8320]{1,0:T(8,128)S(1)}, u32[]{:S(2)}, u32[]{:S(2)}) collective-permute-start(f32[8,8320]{1,0:T(8,128)} %get-tuple-element.28.pm_ref.refs_0_), channel_id=1, source_target_pairs={{0,4},{1,5},{2,6},{3,7},{4,0},{5,1},{6,2},{7,3},{8,12},{9,13},{10,... | collective-permute-start | bytes 798728 | tf_op jit(solution)/shard_map/ppermute | solution.py:519
  8.2 22.6 %collective-permute-start.2 = (f32[8,8320]{1,0:T(8,128)}, f32[8,8320]{1,0:T(8,128)S(1)}, u32[]{:S(2)}, u32[]{:S(2)}) collective-permute-start(f32[8,8320]{1,0:T(8,128)} %get-tuple-element.28.pm_ref.refs_0_), channel_id=1, source_target_pairs={{0,5},{1,4},{2,7},{3,6},{4,1},{5,0},{6,3},{7,2},{8,13},{9,12},{10,... | collective-permute-start | bytes 798728 | tf_op jit(solution)/shard_map/ppermute | solution.py:519
  8.2 11.3 %copy-start.1 = (f32[8,8320]{1,0:T(8,128)S(1)}, f32[8,8320]{1,0:T(8,128)}, u32[]{:S(2)}) copy-start(f32[8,8320]{1,0:T(8,128)} %get-tuple-element.28.pm_ref.refs_0_) | copy-start | bytes 798724
  8.2 11.3 %copy-start.4 = (s32[64,8]{0,1:T(8,128)S(1)}, s32[64,8]{0,1:T(8,128)}, u32[]{:S(2)}) copy-start(s32[64,8]{0,1:T(8,128)} %param.15) | copy-start | bytes 6148
  8.2 28.1 %all-to-all-start = ((f32[128,3,4,128]{3,2,1,0:T(4,128)}), f32[128,3,4,128]{3,2,1,0:T(4,128)S(1)}, u32[]{:S(2)}, u32[]{:S(2)}) async-start(f32[128,3,4,128]{3,2,1,0:T(4,128)} %get-tuple-element.26), calls=%async_computation | async-start | bytes 1572864 | tf_op jit(solution)/shard_map/all_to_all | solution.py:498
  36.3 1.8 %collective-permute-start.3 = (f32[8,8320]{1,0:T(8,128)S(1)}, f32[8,8320]{1,0:T(8,128)S(1)}, u32[]{:S(2)}, u32[]{:S(2)}) collective-permute-start(f32[8,8320]{1,0:T(8,128)S(1)} %copy-done.1), channel_id=1, source_target_pairs={{0,16},{16,0},{32,48},{48,32},{64,80},{80,64},{96,112},{112,96},{1... | collective-permute-start | bytes 798728 | tf_op jit(solution)/shard_map/ppermute | solution.py:522
  37.0 1.7 %collective-permute-start.4 = (f32[8,8320]{1,0:T(8,128)S(1)}, f32[8,8320]{1,0:T(8,128)S(1)}, u32[]{:S(2)}, u32[]{:S(2)}) collective-permute-start(f32[8,8320]{1,0:T(8,128)S(1)} %collective-permute-done.refs_1_), channel_id=1, source_target_pairs={{0,16},{16,0},{32,48},{48,32},{64,80},{80,64},{96,112},{112,96},{1... | collective-permute-start | bytes 798728 | tf_op jit(solution)/shard_map/ppermute | solution.py:522
  37.0 3.3 %collective-permute-start.5 = (f32[8,8320]{1,0:T(8,128)S(1)}, f32[8,8320]{1,0:T(8,128)S(1)}, u32[]{:S(2)}, u32[]{:S(2)}) collective-permute-start(f32[8,8320]{1,0:T(8,128)S(1)} %collective-permute-done.1.refs_2_), channel_id=1, source_target_pairs={{0,16},{16,0},{32,48},{48,32},{64,80},{80,64},{96,112},{112,96},{1... | collective-permute-start | bytes 798728 | tf_op jit(solution)/shard_map/ppermute | solution.py:522
  37.5 2.8 %collective-permute-start.6 = (f32[8,8320]{1,0:T(8,128)S(1)}, f32[8,8320]{1,0:T(8,128)S(1)}, u32[]{:S(2)}, u32[]{:S(2)}) collective-permute-start(f32[8,8320]{1,0:T(8,128)S(1)} %collective-permute-done.2.refs_3_), channel_id=1, source_target_pairs={{0,16},{16,0},{32,48},{48,32},{64,80},{80,64},{96,112},{112,96},{1... | collective-permute-start | bytes 798728 | tf_op jit(solution)/shard_map/ppermute | solution.py:522
  37.5 26.3 %collective-permute-start.7 = (f32[128,4,128]{2,1,0:T(4,128)S(1)}, f32[128,4,128]{2,1,0:T(4,128)S(1)}, u32[]{:S(2)}, u32[]{:S(2)}) collective-permute-start(f32[128,4,128]{2,1,0:T(4,128)S(1)} %slice_bitcast_fusion.refs_0_), channel_id=1, source_target_pairs={{0,1},{1,0},{2,3},{3,2},{4,5},{5,4},{6,7},{7,6},{8,9},{9,8},{10,11... | collective-permute-start | bytes 786440 | tf_op jit(solution)/shard_map/ppermute | solution.py:519
  38.1 25.7 %collective-permute-start.8 = (f32[128,4,128]{2,1,0:T(4,128)S(1)}, f32[128,4,128]{2,1,0:T(4,128)S(1)}, u32[]{:S(2)}, u32[]{:S(2)}) collective-permute-start(f32[128,4,128]{2,1,0:T(4,128)S(1)} %slice_bitcast_fusion.refs_0_), channel_id=1, source_target_pairs={{0,4},{1,5},{2,6},{3,7},{4,0},{5,1},{6,2},{7,3},{8,12},{9,13},{10,... | collective-permute-start | bytes 786440 | tf_op jit(solution)/shard_map/ppermute | solution.py:519
  38.7 25.1 %collective-permute-start.9 = (f32[128,4,128]{2,1,0:T(4,128)S(1)}, f32[128,4,128]{2,1,0:T(4,128)S(1)}, u32[]{:S(2)}, u32[]{:S(2)}) collective-permute-start(f32[128,4,128]{2,1,0:T(4,128)S(1)} %slice_bitcast_fusion.refs_0_), channel_id=1, source_target_pairs={{0,5},{1,4},{2,7},{3,6},{4,1},{5,0},{6,3},{7,2},{8,13},{9,12},{10,... | collective-permute-start | bytes 786440 | tf_op jit(solution)/shard_map/ppermute | solution.py:519
  63.8 11.9 %copy-start.2 = (s32[32,128]{1,0:T(8,128)S(1)}, s32[32,128]{1,0:T(8,128)}, u32[]{:S(2)}) copy-start(s32[32,128]{1,0:T(8,128)} %get-tuple-element.23.row_ref) | copy-start | bytes 49156
  63.8 11.9 %copy-start.3 = (s32[32,128]{1,0:T(8,128)S(1)}, s32[32,128]{1,0:T(8,128)}, u32[]{:S(2)}) copy-start(s32[32,128]{1,0:T(8,128)} %get-tuple-element.24.part_ref) | copy-start | bytes 49156
  63.8 11.8 %collective-permute-start.10 = (f32[128,4,128]{2,1,0:T(4,128)S(1)}, f32[128,4,128]{2,1,0:T(4,128)S(1)}, u32[]{:S(2)}, u32[]{:S(2)}) collective-permute-start(f32[128,4,128]{2,1,0:T(4,128)S(1)} %slice_bitcast_fusion.refs_0_), channel_id=1, source_target_pairs={{0,16},{16,0},{32,48},{48,32},{64,80},{80,64},{96,112},{112,96},{1... | collective-permute-start | bytes 786440 | tf_op jit(solution)/shard_map/ppermute | solution.py:522
  65.0 10.7 %collective-permute-start.11 = (f32[128,4,128]{2,1,0:T(4,128)S(1)}, f32[128,4,128]{2,1,0:T(4,128)S(1)}, u32[]{:S(2)}, u32[]{:S(2)}) collective-permute-start(f32[128,4,128]{2,1,0:T(4,128)S(1)} %collective-permute-done.7.refs_1_), channel_id=1, source_target_pairs={{0,16},{16,0},{32,48},{48,32},{64,80},{80,64},{96,112},{112,96},{1... | collective-permute-start | bytes 786440 | tf_op jit(solution)/shard_map/ppermute | solution.py:522
  65.0 10.6 %collective-permute-start.12 = (f32[128,4,128]{2,1,0:T(4,128)S(1)}, f32[128,4,128]{2,1,0:T(4,128)S(1)}, u32[]{:S(2)}, u32[]{:S(2)}) collective-permute-start(f32[128,4,128]{2,1,0:T(4,128)S(1)} %collective-permute-done.8.refs_2_), channel_id=1, source_target_pairs={{0,16},{16,0},{32,48},{48,32},{64,80},{80,64},{96,112},{112,96},{1... | collective-permute-start | bytes 786440 | tf_op jit(solution)/shard_map/ppermute | solution.py:522
  65.5 10.2 %collective-permute-start.13 = (f32[128,4,128]{2,1,0:T(4,128)S(1)}, f32[128,4,128]{2,1,0:T(4,128)S(1)}, u32[]{:S(2)}, u32[]{:S(2)}) collective-permute-start(f32[128,4,128]{2,1,0:T(4,128)S(1)} %collective-permute-done.9.refs_3_), channel_id=1, source_target_pairs={{0,16},{16,0},{32,48},{48,32},{64,80},{80,64},{96,112},{112,96},{1... | collective-permute-start | bytes 786440 | tf_op jit(solution)/shard_map/ppermute | solution.py:522
  65.6 24.2 %all-to-all-start.1 = ((f32[128,2,4,128]{3,2,1,0:T(4,128)}), f32[128,2,4,128]{3,2,1,0:T(4,128)S(1)}, u32[]{:S(2)}, u32[]{:S(2)}) async-start(f32[128,2,4,128]{3,2,1,0:T(4,128)} %remote_pull.1), calls=%async_computation.1 | async-start | bytes 1048576 | tf_op jit(solution)/shard_map/all_to_all | solution.py:498
  89.7 0.7 copy-start
